TPU v7x, 256 devices: a whole 4x4x8 slice. The times are simulated.
256 devices in a mesh: space: 64 (over z, x, core), sub: 4 (over y).
Axes of the slice: x: 4, y: 4, z: 8, core: 2. Of those that a mesh axis runs over, the one named last changes fastest.
Arguments:
- trajectories: bfloat16 [300, 131072], P(None, ('space', 'sub')), may hold values from -6 to 6
- kernel_scale: bfloat16 [131072], P(('space', 'sub')), may hold values from 6.90625 to 17.25
- start_vectors: float32 [32, 131072], P(None, ('space', 'sub')), may hold values from -6 to 6
- pair_list: int32 [6144, 2], P(('space', 'sub')), may hold values from 0 to 511, as said below
Outputs:
- subspace: float32 [32, 131072], P(None, ('space', 'sub'))
Inputs may be any that keep to these rules, and one draw needn't show every extreme that they name: `pair_list`: pairs in rows k * 12 * 2 to (k + 1) * 12 * 2 - 1 have their row block a in k * 2 to (k + 1) * 2 - 1, k being a device's index along space+sub. Every block appears once as (a, a). For every other pair, b lies on a device whose space index is that of a's device plus 1 to 3, modulo the size of the space axis. No pair appears twice.
All inputs are finite; a program needn't handle non-finite values.
Results may differ from a plain program's by a relative error of at most 0.0041.
Values may be sent and summed in bfloat16 or wider, within the bound.
No kernel may reach another device: no remote copies, remote signals or barrier semaphores. Data moves between devices by JAX's collectives and lax.ppermute only.
A program may use at most 64 MiB of HBM per device.

v0:
```python
import jax
import jax.numpy as jnp
from jax import lax
from jax.sharding import PartitionSpec as P

FEAT = 300
BLOCK = 256
REACH = 3
ITERS = 2


def passed_along(value, axis, steps):
    count = lax.axis_size(axis)
    pairs = [(source, (source + steps) % count) for source in range(count)]
    return lax.ppermute(value, axis, pairs)


def local_blocks(source):
    chans = source.shape[0]
    count = source.shape[1] // BLOCK
    return source.reshape(chans, count, BLOCK).transpose(1, 0, 2)


def near_blocks(nearby):
    reach, n_sub, chans, length = nearby.shape
    count = length // BLOCK
    shaped = nearby.reshape(reach, n_sub, chans, count, BLOCK).transpose(0, 1, 3, 2, 4)
    return shaped.reshape(reach * n_sub * count, chans, BLOCK)


def candidates(local, nearby):
    return jnp.concatenate([local_blocks(local), near_blocks(nearby)], 0)


def batch_similarity(row_data, col_data):
    row_coord = row_data[:, :FEAT, :]
    col_coord = col_data[:, :FEAT, :]
    crossed = jnp.einsum("pfi,pfj->pij", row_coord, col_coord, preferred_element_type=jnp.float32)
    row_norms = jnp.sum(jnp.square(row_coord.astype(jnp.float32)), 1)
    col_norms = jnp.sum(jnp.square(col_coord.astype(jnp.float32)), 1)
    scaling = (
        row_data[:, FEAT, :].astype(jnp.float32)[:, :, None]
        * col_data[:, FEAT, :].astype(jnp.float32)[:, None, :]
    )
    spread = row_norms[:, :, None] + col_norms[:, None, :] - 2.0 * crossed
    return jnp.exp(-spread / scaling).astype(jnp.bfloat16)


def nearby_vectors(scaled):
    whole = lax.all_gather(scaled[None], "sub", axis=0, tiled=True)
    return jnp.stack(
        [passed_along(whole, "space", -hop_count) for hop_count in range(1, REACH + 1)]
    )


def return_far(acc_far):
    returned = jnp.zeros(acc_far.shape[1:], jnp.float32)
    for hop_count in range(1, REACH + 1):
        returned = returned + passed_along(acc_far[hop_count - 1], "space", hop_count)
    return lax.psum_scatter(returned, "sub", scatter_dimension=0, tiled=True)[0]


def on_device(trajectories, kernel_scale, start_vectors, pair_list):
    length = trajectories.shape[1]
    blocks = length // BLOCK
    n_sub = lax.axis_size("sub")
    n_space = lax.axis_size("space")
    space_at = lax.axis_index("space")
    sub_at = lax.axis_index("sub")
    packed = jnp.concatenate([trajectories, kernel_scale[None, :]], 0)
    whole = lax.all_gather(packed[None], "sub", axis=0, tiled=True)
    near_traj = jnp.stack(
        [passed_along(whole, "space", -hop_count) for hop_count in range(1, REACH + 1)]
    )
    row_blk = pair_list[:, 0] - (space_at * n_sub + sub_at) * blocks
    col_ids = pair_list[:, 1]
    col_dev = col_ids // blocks
    col_blk = col_ids % blocks
    col_sub = col_dev % n_sub
    offset = jnp.remainder(col_dev // n_sub - space_at, n_space)
    far_slot = jnp.maximum(offset - 1, 0)
    far_index = (far_slot * n_sub + col_sub) * blocks + col_blk
    is_far = offset > 0
    cand_index = jnp.where(is_far, blocks + far_index, col_blk)
    far_total = REACH * n_sub * blocks
    row_onehot = (row_blk[:, None] == jnp.arange(blocks, dtype=jnp.int32)[None, :]).astype(
        jnp.float32
    )
    far_onehot = (
        (far_index[:, None] == jnp.arange(far_total, dtype=jnp.int32)[None, :]) & is_far[:, None]
    ).astype(jnp.float32)
    traj_table = candidates(packed, near_traj)
    own_traj = local_blocks(packed)

    def make_tiles():
        row_data = jnp.take(own_traj, row_blk, axis=0)
        col_data = jnp.take(traj_table, cand_index, axis=0)
        return batch_similarity(row_data, col_data)

    def sweep(local, nearby, weights_tiles):
        vec_count = local.shape[0]
        vec_table = candidates(local, nearby)
        left_vec = jnp.take(local_blocks(local), row_blk, axis=0)
        right_vec = jnp.take(vec_table, cand_index, axis=0)
        row_term = jnp.einsum(
            "pvj,pij->pvi", right_vec, weights_tiles, preferred_element_type=jnp.float32
        )
        col_term = jnp.einsum(
            "pvi,pij->pvj", left_vec, weights_tiles, preferred_element_type=jnp.float32
        )
        row_sum = jnp.einsum(
            "pb,pvi->bvi",
            row_onehot,
            row_term,
            precision=lax.Precision.HIGHEST,
            preferred_element_type=jnp.float32,
        )
        far_sum = jnp.einsum(
            "pk,pvj->kvj",
            far_onehot,
            col_term,
            precision=lax.Precision.HIGHEST,
            preferred_element_type=jnp.float32,
        )
        acc_row = row_sum.transpose(1, 0, 2).reshape(vec_count, length)
        acc_far = (
            far_sum.reshape(REACH, n_sub, blocks, vec_count, BLOCK)
            .transpose(0, 1, 3, 2, 4)
            .reshape(REACH, n_sub, vec_count, length)
        )
        return acc_row + return_far(acc_far)

    first_tiles = make_tiles()
    ones_local = jnp.ones((1, length), jnp.bfloat16)
    ones_near = jnp.ones((REACH, n_sub, 1, length), jnp.bfloat16)
    degree = sweep(ones_local, ones_near, first_tiles)
    inverse_root = lax.rsqrt(degree[0])
    vectors = start_vectors
    for sweep_turn in range(ITERS):
        scaled = (inverse_root[None, :] * vectors).astype(jnp.bfloat16)
        weights_tiles = make_tiles()
        image_sum = sweep(scaled, nearby_vectors(scaled), weights_tiles)
        image = inverse_root[None, :] * image_sum
        gram = lax.psum(
            jnp.dot(
                image, image.T, precision=lax.Precision.HIGHEST, preferred_element_type=jnp.float32
            ),
            ("space", "sub"),
        )
        factor = jnp.linalg.cholesky(gram)
        vectors = lax.linalg.triangular_solve(factor, image, left_side=True, lower=True)
    return vectors


def solution(mesh):
    placed = (
        P(None, ("space", "sub")),
        P(("space", "sub")),
        P(None, ("space", "sub")),
        P(("space", "sub"), None),
    )
    return jax.shard_map(
        on_device, mesh=mesh, in_specs=placed, out_specs=P(None, ("space", "sub")), check_vma=False
    )
```

profile of v0, /device:TPU:1, one launch (start us, length us, event | category | flops | bytes accessed | tf_op | source)
XLA Modules:
  0.0 479.4 jit_solution(9813021109696625887)
XLA Ops:
  7.2 1.7 maximum_bitcast_fusion.4
  12.5 26.7 %all-gather.6.cloned.1.call-done = bf16[4,301,512]{2,1,0:T(8,128)(2,1)} async-done(((bf16[1,301,512]{2,1,0:T(8,128)(2,1)}), bf16[4,301,512]{2,1,0:T(8,128)(2,1)}) %all-gather.6.cloned.1.call-update) | async-done | bytes 1232912 | tf_op jit(solution)/shard_map/all_gather | solution.py:71
  39.2 3.4 copy.69
  42.5 6.8 %collective-permute-start.2 = (bf16[4,301,512]{2,0,1:T(4,128)(2,1)}, bf16[4,301,512]{2,0,1:T(4,128)(2,1)S(1)}, u32[]{:S(2)}, u32[]{:S(2)}) collective-permute-start(bf16[4,301,512]{2,0,1:T(4,128)(2,1)} %copy.69), channel_id=1, source_target_pairs={{0,244},{4,248},{8,252},{12,0},{16,4},{20,8},{24,12},{28,16},{32,2... | collective-permute-start | bytes 3698696 | tf_op jit(solution)/shard_map/ppermute | solution.py:15
  50.1 2.7 gather_fusion.2
  54.9 2.5 broadcast_select_fusion.1
  57.4 1.8 copy-done
  59.2 17.4 %collective-permute-done.2 = bf16[4,301,512]{2,0,1:T(4,128)(2,1)S(1)} collective-permute-done((bf16[4,301,512]{2,0,1:T(4,128)(2,1)}, bf16[4,301,512]{2,0,1:T(4,128)(2,1)S(1)}, u32[]{:S(2)}, u32[]{:S(2)}) %collective-permute-start.2) | collective-permute-done | bytes 1232928 | tf_op jit(solution)/shard_map/ppermute | solution.py:15
  77.0 33.9 %collective-permute-done.1 = bf16[4,301,512]{2,0,1:T(4,128)(2,1)} collective-permute-done((bf16[4,301,512]{2,0,1:T(4,128)(2,1)}, bf16[4,301,512]{2,0,1:T(4,128)(2,1)}, u32[]{:S(2)}, u32[]{:S(2)}) %collective-permute-start.1) | collective-permute-done | bytes 1232928 | tf_op jit(solution)/shard_map/ppermute | solution.py:15
  110.9 3.1 reshape.321
  114.0 4.0 reshape.320
  118.0 7.2 %maximum_bitcast_fusion = bf16[3,4,2,301,256]{4,2,1,3,0:T(2,128)(2,1)S(1)} fusion(bf16[1,4,301,2,256]{4,3,1,2,0:T(2,128)(2,1)S(1)} %reshape.322, bf16[1,4,301,2,256]{4,3,1,2,0:T(2,128)(2,1)S(1)} %reshape.321, bf16[1,4,301,2,256]{4,3,1,2,0:T(2,128)(2,1)} %reshape.320), kind=kLoop, calls=%fused_computation.14 | loop fusion | flops 3698688 | bytes 7397376 | tf_op jit(solution)/shard_map/transpose | solution.py:27
  126.0 2.3 pad_maximum_fusion
  128.3 5.0 %gather_fusion.3 = bf16[24,301,256]{2,1,0:T(8,128)(2,1)} fusion(bf16[26,301,256]{2,1,0:T(8,128)(2,1)} %pad_maximum_fusion, s32[1024]{0:T(1024)S(1)} %pad_clamp_fusion.1), kind=kCustom, calls=%fused_computation.1.clone | custom fusion | bytes 7397472 | tf_op jit(solution)/shard_map/jit(_take)/gather | solution.py:97
  133.3 2.6 broadcast_select_fusion
  138.0 4.1 exponential_convert_fusion
  145.3 4.5 collective-permute-start.4
  150.3 1.8 collective-permute-done.4
  152.1 8.0 %all-reduce = f32[4,1,512]{2,1,0:T(1,128)S(1)} all-reduce(f32[4,1,512]{2,1,0:T(1,128)S(1)} %add_add_fusion.2), channel_id=5, replica_groups=mesh['space'=64,'sub'=4] {'sub'}, use_global_device_ids=true, to_apply=%region_2.5.clone | all-reduce | flops 2048 | bytes 16384
  162.0 9.8 %all-gather.1 = bf16[128,512]{1,0:T(8,128)(2,1)} all-gather(bf16[32,512]{1,0:T(8,128)(2,1)S(1)} %multiply_convert_fusion), channel_id=3, replica_groups=mesh['space'=64,'sub'=4] {'sub'}, dimensions={0}, use_global_device_ids=true | all-gather | bytes 163840 | tf_op jit(solution)/shard_map/all_gather | solution.py:50
  171.8 8.0 %collective-permute-start.8 = (bf16[4,32,512]{2,1,0:T(8,128)(2,1)}, bf16[4,32,512]{2,1,0:T(8,128)(2,1)}, u32[]{:S(2)}, u32[]{:S(2)}) collective-permute-start(bf16[4,32,512]{2,1,0:T(8,128)(2,1)} %bitcast.20), channel_id=1, source_target_pairs={{0,244},{4,248},{8,252},{12,0},{16,4},{20,8},{24,12},{28,16},{32,2... | collective-permute-start | bytes 393224 | tf_op jit(solution)/shard_map/ppermute | solution.py:15
  184.2 1.9 fusion.12
  186.0 2.5 reshape.204
  188.5 2.1 fusion.88
  192.6 2.2 collective-permute-start.11
  204.7 1.7 gather_fusion.4
  206.4 6.8 %collective-permute-done.10 = f32[4,32,512]{2,1,0:T(8,128)} collective-permute-done((f32[4,32,512]{2,1,0:T(8,128)}, f32[4,32,512]{2,1,0:T(8,128)}, u32[]{:S(2)}, u32[]{:S(2)}) %collective-permute-start.10) | collective-permute-done | bytes 262176 | tf_op jit(solution)/shard_map/ppermute | solution.py:15
  213.3 1.9 add_add_fusion.1
  215.2 1.7 fusion.22
  218.4 11.9 %reduce-scatter.3.cloned.1.call-done = f32[1,32,512]{2,1,0:T(8,128)} async-done(((f32[4,32,512]{2,1,0:T(8,128)}), f32[1,32,512]{2,1,0:T(8,128)}) %reduce-scatter.3.cloned.1.call-update) | async-done | bytes 65552 | tf_op jit(solution)/shard_map/reduce_scatter | solution.py:60
  231.4 78.2 %psum.14 = f32[32,32]{0,1:T(8,128)S(1)} all-reduce(f32[32,32]{0,1:T(8,128)S(1)} %convolution_bitcast_fusion.1), channel_id=1, replica_groups=mesh['space'=64,'sub'=4] {'space','sub'}, use_global_device_ids=true, to_apply=%region_4.9 | all-reduce | flops 1024 | bytes 8192 | tf_op jit(solution)/shard_map/psum | solution.py:144
  309.7 2.9 cholesky.44
  313.9 2.4 custom-call.6
  317.5 9.8 %all-gather.2 = bf16[128,512]{1,0:T(8,128)(2,1)} all-gather(bf16[32,512]{1,0:T(8,128)(2,1)S(1)} %fusion.7), channel_id=4, replica_groups=mesh['space'=64,'sub'=4] {'sub'}, dimensions={0}, use_global_device_ids=true | all-gather | bytes 163840 | tf_op jit(solution)/shard_map/all_gather | solution.py:50
  327.4 5.5 %collective-permute-start.14 = (bf16[4,32,512]{2,1,0:T(8,128)(2,1)}, bf16[4,32,512]{2,1,0:T(8,128)(2,1)}, u32[]{:S(2)}, u32[]{:S(2)}) collective-permute-start(bf16[4,32,512]{2,1,0:T(8,128)(2,1)} %bitcast.32), channel_id=1, source_target_pairs={{0,244},{4,248},{8,252},{12,0},{16,4},{20,8},{24,12},{28,16},{32,2... | collective-permute-start | bytes 393224 | tf_op jit(solution)/shard_map/ppermute | solution.py:15
  337.1 1.8 fusion.8
  339.0 2.5 reshape.208
  344.1 1.9 squeeze.66
  345.9 2.3 collective-permute-start.17
  348.3 1.9 squeeze.64
  356.9 1.7 gather_fusion.6
  358.9 7.7 %collective-permute-done.16 = f32[4,32,512]{2,1,0:T(8,128)} collective-permute-done((f32[4,32,512]{2,1,0:T(8,128)}, f32[4,32,512]{2,1,0:T(8,128)}, u32[]{:S(2)}, u32[]{:S(2)}) %collective-permute-start.16) | collective-permute-done | bytes 262176 | tf_op jit(solution)/shard_map/ppermute | solution.py:15
  366.6 1.9 add_add_fusion
  370.4 14.3 %reduce-scatter.5.cloned.1.call-done = f32[1,32,512]{2,1,0:T(8,128)} async-done(((f32[4,32,512]{2,1,0:T(8,128)}), f32[1,32,512]{2,1,0:T(8,128)}) %reduce-scatter.5.cloned.1.call-update) | async-done | bytes 65552 | tf_op jit(solution)/shard_map/reduce_scatter | solution.py:60
  385.8 78.1 %psum.15 = f32[32,32]{0,1:T(8,128)S(1)} all-reduce(f32[32,32]{0,1:T(8,128)S(1)} %convolution_bitcast_fusion), channel_id=1, replica_groups=mesh['space'=64,'sub'=4] {'space','sub'}, use_global_device_ids=true, to_apply=%region_8.15 | all-reduce | flops 1024 | bytes 8192 | tf_op jit(solution)/shard_map/psum | solution.py:144
  464.0 2.9 cholesky.55
  468.2 2.4 custom-call.7
  470.7 1.8 fusion.33
  (145 shorter events, 55.5 us)
Async XLA Ops:
  6.5 32.6 %all-gather.6.cloned.1.call-start = ((), (), s32[]{:S(2)}) async-start(), calls=%async_computation.4 | async-start | bytes 1556480 | tf_op jit(solution)/shard_map/all_gather | solution.py:71
  9.0 221.3 %reduce-scatter.3.cloned.1.call-start = ((), (), s32[]{:S(2)}) async-start(), calls=%async_computation.2 | async-start | bytes 327680 | tf_op jit(solution)/shard_map/reduce_scatter | solution.py:60
  11.6 138.2 %copy-start.3 = (s32[24,1]{0,1:T(1,128)}, s32[24,1]{0,1:T(1,128)S(1)}, u32[]{:S(2)}) copy-start(s32[24,1]{0,1:T(1,128)S(1)} %get-tuple-element.34) | copy-start | bytes 292
  11.6 169.5 %copy-start.8 = (s32[1024]{0:T(1024)}, s32[1024]{0:T(1024)S(1)}, u32[]{:S(2)}) copy-start(s32[1024]{0:T(1024)S(1)} %pad_clamp_fusion.2) | copy-start | bytes 12292
  11.7 170.8 %copy-start.9 = (pred[24]{0:T(512)(128)(4,1)}, pred[24]{0:T(512)(128)(4,1)S(1)}, u32[]{:S(2)}) copy-start(pred[24]{0:T(512)(128)(4,1)S(1)} %compare_and_fusion.1) | copy-start | bytes 76
  12.5 120.8 %copy-start.5 = (pred[24]{0:T(512)(128)(4,1)}, pred[24]{0:T(512)(128)(4,1)S(1)}, u32[]{:S(2)}) copy-start(pred[24]{0:T(512)(128)(4,1)S(1)} %get-tuple-element.22) | copy-start | bytes 76
  42.5 34.0 %collective-permute-start.2 = (bf16[4,301,512]{2,0,1:T(4,128)(2,1)}, bf16[4,301,512]{2,0,1:T(4,128)(2,1)S(1)}, u32[]{:S(2)}, u32[]{:S(2)}) collective-permute-start(bf16[4,301,512]{2,0,1:T(4,128)(2,1)} %copy.69), channel_id=1, source_target_pairs={{0,244},{4,248},{8,252},{12,0},{16,4},{20,8},{24,12},{28,16},{32,2... | collective-permute-start | bytes 3698696 | tf_op jit(solution)/shard_map/ppermute | solution.py:15
  49.3 61.6 %collective-permute-start.1 = (bf16[4,301,512]{2,0,1:T(4,128)(2,1)}, bf16[4,301,512]{2,0,1:T(4,128)(2,1)}, u32[]{:S(2)}, u32[]{:S(2)}) collective-permute-start(bf16[4,301,512]{2,0,1:T(4,128)(2,1)} %copy.69), channel_id=1, source_target_pairs={{0,248},{4,252},{8,0},{12,4},{16,8},{20,12},{24,16},{28,20},{32,24... | collective-permute-start | bytes 3698696 | tf_op jit(solution)/shard_map/ppermute | solution.py:15
  49.9 64.1 %collective-permute-start = (bf16[4,301,512]{2,0,1:T(4,128)(2,1)}, bf16[4,301,512]{2,0,1:T(4,128)(2,1)}, u32[]{:S(2)}, u32[]{:S(2)}) collective-permute-start(bf16[4,301,512]{2,0,1:T(4,128)(2,1)} %copy.69), channel_id=1, source_target_pairs={{0,252},{4,0},{8,4},{12,8},{16,12},{20,16},{24,20},{28,24},{32,28}... | collective-permute-start | bytes 3698696 | tf_op jit(solution)/shard_map/ppermute | solution.py:15
  50.1 4.0 copy-start.10
  54.7 73.6 %copy-start.7 = (s32[1024]{0:T(1024)}, s32[1024]{0:T(1024)S(1)}, u32[]{:S(2)}) copy-start(s32[1024]{0:T(1024)S(1)} %pad_clamp_fusion.1) | copy-start | bytes 12292
  57.4 1.8 copy-start
  133.3 3.2 copy-start.1
  142.2 19.8 %copy-start.2 = (f32[32,512]{1,0:T(8,128)S(1)}, f32[32,512]{1,0:T(8,128)}, u32[]{:S(2)}) copy-start(f32[32,512]{1,0:T(8,128)} %param.17) | copy-start | bytes 196612
  143.8 6.5 %collective-permute-start.5 = (f32[4,1,512]{2,1,0:T(1,128)S(1)}, f32[4,1,512]{2,1,0:T(1,128)S(1)}, u32[]{:S(2)}, u32[]{:S(2)}) collective-permute-start(f32[4,1,512]{2,1,0:T(1,128)S(1)} %squeeze.71), channel_id=1, source_target_pairs={{0,12},{4,16},{8,20},{12,24},{16,28},{20,32},{24,36},{28,40},{32,4... | collective-permute-start | bytes 24584 | tf_op jit(solution)/shard_map/ppermute | solution.py:15
  144.2 6.1 %collective-permute-start.3 = (f32[4,1,512]{2,1,0:T(1,128)S(1)}, f32[4,1,512]{2,1,0:T(1,128)S(1)}, u32[]{:S(2)}, u32[]{:S(2)}) collective-permute-start(f32[4,1,512]{2,1,0:T(1,128)S(1)} %squeeze.69), channel_id=1, source_target_pairs={{0,4},{4,8},{8,12},{12,16},{16,20},{20,24},{24,28},{28,32},{32,36}... | collective-permute-start | bytes 24584 | tf_op jit(solution)/shard_map/ppermute | solution.py:15
  145.3 6.8 %collective-permute-start.4 = (f32[4,1,512]{2,1,0:T(1,128)S(1)}, f32[4,1,512]{2,1,0:T(1,128)S(1)}, u32[]{:S(2)}, u32[]{:S(2)}) collective-permute-start(f32[4,1,512]{2,1,0:T(1,128)S(1)} %squeeze.70), channel_id=1, source_target_pairs={{0,8},{4,12},{8,16},{12,20},{16,24},{20,28},{24,32},{28,36},{32,40... | collective-permute-start | bytes 24584 | tf_op jit(solution)/shard_map/ppermute | solution.py:15
  171.8 26.9 %collective-permute-start.8 = (bf16[4,32,512]{2,1,0:T(8,128)(2,1)}, bf16[4,32,512]{2,1,0:T(8,128)(2,1)}, u32[]{:S(2)}, u32[]{:S(2)}) collective-permute-start(bf16[4,32,512]{2,1,0:T(8,128)(2,1)} %bitcast.20), channel_id=1, source_target_pairs={{0,244},{4,248},{8,252},{12,0},{16,4},{20,8},{24,12},{28,16},{32,2... | collective-permute-start | bytes 393224 | tf_op jit(solution)/shard_map/ppermute | solution.py:15
  179.8 19.9 %collective-permute-start.7 = (bf16[4,32,512]{2,1,0:T(8,128)(2,1)}, bf16[4,32,512]{2,1,0:T(8,128)(2,1)}, u32[]{:S(2)}, u32[]{:S(2)}) collective-permute-start(bf16[4,32,512]{2,1,0:T(8,128)(2,1)} %bitcast.20), channel_id=1, source_target_pairs={{0,248},{4,252},{8,0},{12,4},{16,8},{20,12},{24,16},{28,20},{32,24... | collective-permute-start | bytes 393224 | tf_op jit(solution)/shard_map/ppermute | solution.py:15
  181.1 19.5 %collective-permute-start.6 = (bf16[4,32,512]{2,1,0:T(8,128)(2,1)}, bf16[4,32,512]{2,1,0:T(8,128)(2,1)}, u32[]{:S(2)}, u32[]{:S(2)}) collective-permute-start(bf16[4,32,512]{2,1,0:T(8,128)(2,1)} %bitcast.20), channel_id=1, source_target_pairs={{0,252},{4,0},{8,4},{12,8},{16,12},{20,16},{24,20},{28,24},{32,28}... | collective-permute-start | bytes 393224 | tf_op jit(solution)/shard_map/ppermute | solution.py:15
  192.6 13.8 %collective-permute-start.11 = (f32[4,32,512]{2,1,0:T(8,128)}, f32[4,32,512]{2,1,0:T(8,128)}, u32[]{:S(2)}, u32[]{:S(2)}) collective-permute-start(f32[4,32,512]{2,1,0:T(8,128)} %copy.112), channel_id=1, source_target_pairs={{0,12},{4,16},{8,20},{12,24},{16,28},{20,32},{24,36},{28,40},{32,4... | collective-permute-start | bytes 786440 | tf_op jit(solution)/shard_map/ppermute | solution.py:15
  196.8 9.6 %collective-permute-start.9 = (f32[4,32,512]{2,1,0:T(8,128)}, f32[4,32,512]{2,1,0:T(8,128)}, u32[]{:S(2)}, u32[]{:S(2)}) collective-permute-start(f32[4,32,512]{2,1,0:T(8,128)} %copy.110), channel_id=1, source_target_pairs={{0,4},{4,8},{8,12},{12,16},{16,20},{20,24},{24,28},{28,32},{32,36}... | collective-permute-start | bytes 786440 | tf_op jit(solution)/shard_map/ppermute | solution.py:15
  198.8 14.5 %collective-permute-start.10 = (f32[4,32,512]{2,1,0:T(8,128)}, f32[4,32,512]{2,1,0:T(8,128)}, u32[]{:S(2)}, u32[]{:S(2)}) collective-permute-start(f32[4,32,512]{2,1,0:T(8,128)} %copy.111), channel_id=1, source_target_pairs={{0,8},{4,12},{8,16},{12,20},{16,24},{20,28},{24,32},{28,36},{32,40... | collective-permute-start | bytes 786440 | tf_op jit(solution)/shard_map/ppermute | solution.py:15
  215.1 169.5 %reduce-scatter.5.cloned.1.call-start = ((), (), s32[]{:S(2)}) async-start(), calls=%async_computation.3 | async-start | bytes 327680 | tf_op jit(solution)/shard_map/reduce_scatter | solution.py:60
  327.4 23.7 %collective-permute-start.14 = (bf16[4,32,512]{2,1,0:T(8,128)(2,1)}, bf16[4,32,512]{2,1,0:T(8,128)(2,1)}, u32[]{:S(2)}, u32[]{:S(2)}) collective-permute-start(bf16[4,32,512]{2,1,0:T(8,128)(2,1)} %bitcast.32), channel_id=1, source_target_pairs={{0,244},{4,248},{8,252},{12,0},{16,4},{20,8},{24,12},{28,16},{32,2... | collective-permute-start | bytes 393224 | tf_op jit(solution)/shard_map/ppermute | solution.py:15
  332.8 19.2 %collective-permute-start.13 = (bf16[4,32,512]{2,1,0:T(8,128)(2,1)}, bf16[4,32,512]{2,1,0:T(8,128)(2,1)}, u32[]{:S(2)}, u32[]{:S(2)}) collective-permute-start(bf16[4,32,512]{2,1,0:T(8,128)(2,1)} %bitcast.32), channel_id=1, source_target_pairs={{0,248},{4,252},{8,0},{12,4},{16,8},{20,12},{24,16},{28,20},{32,24... | collective-permute-start | bytes 393224 | tf_op jit(solution)/shard_map/ppermute | solution.py:15
  334.0 18.9 %collective-permute-start.12 = (bf16[4,32,512]{2,1,0:T(8,128)(2,1)}, bf16[4,32,512]{2,1,0:T(8,128)(2,1)}, u32[]{:S(2)}, u32[]{:S(2)}) collective-permute-start(bf16[4,32,512]{2,1,0:T(8,128)(2,1)} %bitcast.32), channel_id=1, source_target_pairs={{0,252},{4,0},{8,4},{12,8},{16,12},{20,16},{24,20},{28,24},{32,28}... | collective-permute-start | bytes 393224 | tf_op jit(solution)/shard_map/ppermute | solution.py:15
  344.1 24.4 %copy-start.6 = (pred[24]{0:T(512)(128)(4,1)S(1)}, pred[24]{0:T(512)(128)(4,1)}, u32[]{:S(2)}) copy-start(pred[24]{0:T(512)(128)(4,1)} %copy-done.5) | copy-start | bytes 76
  345.9 12.7 %collective-permute-start.17 = (f32[4,32,512]{2,1,0:T(8,128)}, f32[4,32,512]{2,1,0:T(8,128)}, u32[]{:S(2)}, u32[]{:S(2)}) collective-permute-start(f32[4,32,512]{2,1,0:T(8,128)} %squeeze.66), channel_id=1, source_target_pairs={{0,12},{4,16},{8,20},{12,24},{16,28},{20,32},{24,36},{28,40},{32,4... | collective-permute-start | bytes 786440 | tf_op jit(solution)/shard_map/ppermute | solution.py:15
  350.1 8.7 %collective-permute-start.15 = (f32[4,32,512]{2,1,0:T(8,128)}, f32[4,32,512]{2,1,0:T(8,128)}, u32[]{:S(2)}, u32[]{:S(2)}) collective-permute-start(f32[4,32,512]{2,1,0:T(8,128)} %squeeze.64), channel_id=1, source_target_pairs={{0,4},{4,8},{8,12},{12,16},{16,20},{20,24},{24,28},{28,32},{32,36}... | collective-permute-start | bytes 786440 | tf_op jit(solution)/shard_map/ppermute | solution.py:15
  351.0 15.6 %collective-permute-start.16 = (f32[4,32,512]{2,1,0:T(8,128)}, f32[4,32,512]{2,1,0:T(8,128)}, u32[]{:S(2)}, u32[]{:S(2)}) collective-permute-start(f32[4,32,512]{2,1,0:T(8,128)} %squeeze.65), channel_id=1, source_target_pairs={{0,8},{4,12},{8,16},{12,20},{16,24},{20,28},{24,32},{28,36},{32,40... | collective-permute-start | bytes 786440 | tf_op jit(solution)/shard_map/ppermute | solution.py:15
  356.1 13.4 %copy-start.4 = (s32[24,1]{0,1:T(1,128)S(1)}, s32[24,1]{0,1:T(1,128)}, u32[]{:S(2)}) copy-start(s32[24,1]{0,1:T(1,128)} %copy-done.3) | copy-start | bytes 292
Sparse Core Ops, SparseCore 0:
  9.2 29.9 all-gather.5
  215.3 14.9 reduce-scatter.2
  368.6 16.0 reduce-scatter.4
where the time goes:
time: 484 us; the launch traced here: 479 us
  blocking collectives  184 us (38%)
  waiting for transfers between devices  121 us (25%)
  local copies, waits for them, and re-layouts  63.5 us (13%)
  other arithmetic  41.6 us (9%)
  starting transfers between devices  34.1 us (7%)
  matrix products  21.1 us (4%)
  between operations  14.2 us (3%)
    psum x2, blocking collectives, on_device(): lax.psum(jnp.dot(image, image.T, precision=lax.Precision.HIGHEST, preferr...  156 us
    ppermute x18, waiting for transfers between devices, passed_along(): return lax.ppermute(value, axis, pairs)  68.1 us
    ppermute x18, starting transfers between devices, passed_along(): return lax.ppermute(value, axis, pairs)  34 us
    all_gather x1, waiting for transfers between devices, on_device(): whole = lax.all_gather(packed[None], 'sub', axis=0, tiled=True)  26.7 us
    reduce_scatter x2, waiting for transfers between devices, return_far(): return lax.psum_scatter(returned, 'sub', scatter_dimension=0, tiled=True)[0]  26.2 us
    all_gather x2, blocking collectives, nearby_vectors(): whole = lax.all_gather(scaled[None], 'sub', axis=0, tiled=True)  19.7 us
    squeeze x12, local copies, waits for them, and re-layouts, return_far(): acc_far[hop_count - 1]  10.6 us
    transpose x3, other arithmetic, near_blocks(): nearby.reshape(reach, n_sub, chans, count, BLOCK).transpose(0, 1, 3, 2, 4)  10.3 us
  transfers between devices with their start and end apart: 21, of which 10 were waited for; matrix products, arithmetic and copies ran while one was open for 13% of the time, Pallas kernels for 0%

commit v1 on v0

v1 whole, which is shorter than its diff:
```python
import functools

import jax
import jax.numpy as jnp
from jax import lax
from jax.experimental import pallas as pl
from jax.experimental.pallas import tpu as pltpu
from jax.sharding import PartitionSpec as P

FEAT = 300
BLOCK = 256
REACH = 3
ROWS = 304
SCALE_ROW = 300
MASK_ROW = 301
MASKED = 1e30
LOG2E = 1.4426950408889634
VMEM_LIMIT = 48 * 1024 * 1024
TRANS_B = (((1,), (1,)), ((), ()))


def shifted(value, axis, steps):
    count = lax.axis_size(axis)
    return lax.ppermute(value, axis, [((at + steps) % count, at) for at in range(count)])


def window(value):
    group = jnp.stack([value] + [shifted(value, "sub", e) for e in range(1, 4)])
    ahead = {h: shifted(group, "space", h) for h in range(1, REACH + 1)}
    behind = {h: shifted(group, "space", -h) for h in range(1, REACH + 1)}
    return group, ahead, behind


def window_relayed(value):
    group = jnp.stack([value] + [shifted(value, "sub", e) for e in range(1, 4)])
    ahead = {h: shifted(group, "space", h) for h in (1, 2)}
    behind = {h: shifted(group, "space", -h) for h in (1, 2)}
    ahead[3] = shifted(ahead[2], "space", 1)
    behind[3] = shifted(behind[2], "space", -1)
    return group, ahead, behind


def summed(value):
    for axis, stride in (("sub", 1), ("space", 1), ("space", 4), ("space", 16)):
        parts = [shifted(value, axis, stride * k) for k in range(1, 4)]
        value = (value + parts[0]) + (parts[1] + parts[2])
    return value


def squares_of(coords):
    wide = coords.astype(jnp.float32)
    return jnp.sum(wide * wide, axis=0, keepdims=True)


def degree_of(tile):
    ones = jnp.ones((8, tile.shape[1]), jnp.bfloat16)
    return lax.dot_general(ones, tile, TRANS_B, preferred_element_type=jnp.float32)


def tile_rows(lhs, rhs, row_norm, col_norm, row_rate, col_rate):
    crossed = jnp.dot(lhs, rhs, preferred_element_type=jnp.float32)
    spread = crossed - (row_norm + col_norm)
    return jnp.exp2(spread * row_rate * col_rate).astype(jnp.bfloat16)


def bias_rows(used_ref, base, step_r, step_c):
    first = lax.broadcasted_iota(jnp.int32, (1, 2 * BLOCK), 1) < BLOCK
    rows = []
    for r in range(2):
        left, right = (
            jnp.where(used_ref[base + r * step_r + c * step_c] > 0.0, 0.0, MASKED) for c in range(2)
        )
        rows.append(jnp.where(first, left, right))
    return rows


def tile_kernel(mine_ref, theirs_ref, lhs_ref, rate_ref, norm_ref, ahead_ref, behind_ref, tile_ref, degree_ref):
    at = pl.program_id(0)

    @pl.when(at == 0)
    def _():
        degree_ref[...] = jnp.zeros_like(degree_ref)

    biases = (
        bias_rows(mine_ref, at * 4, 2, 1),
        bias_rows(theirs_ref, at * 16 + lax.rem(4 - at, 4) * 4, 1, 2),
    )
    for side, data_ref in enumerate((ahead_ref, behind_ref)):
        data = data_ref[0]
        col_norm = squares_of(data[:FEAT])
        col_rate = 1.0 / data[SCALE_ROW : SCALE_ROW + 1].astype(jnp.float32)
        for r in range(2):
            rows = pl.ds(r * BLOCK, BLOCK)
            tile = tile_rows(
                lhs_ref[rows, :], data, norm_ref[rows, :], col_norm + biases[side][r], rate_ref[rows, :], col_rate
            )
            tile_ref[0, side, rows, :] = tile
            degree_ref[:, rows] += degree_of(tile)


def self_kernel(lhs_ref, rate_ref, norm_ref, own_ref, tile_ref, degree_ref):
    data = own_ref[...]
    col_norm = squares_of(data[:FEAT])
    col_rate = 1.0 / data[SCALE_ROW : SCALE_ROW + 1].astype(jnp.float32)
    first = lax.broadcasted_iota(jnp.int32, (1, 2 * BLOCK), 1) < BLOCK
    for r in range(2):
        bias = jnp.where(first == (r == 0), 0.0, MASKED)
        rows = pl.ds(r * BLOCK, BLOCK)
        tile = tile_rows(
            lhs_ref[rows, :], data, norm_ref[rows, :], col_norm + bias, rate_ref[rows, :], col_rate
        )
        tile_ref[rows, :] = tile
        degree_ref[:, rows] = degree_of(tile)


def whole(shape):
    return pl.BlockSpec(shape, lambda *at: (0,) * len(shape))


def hop_tiles(mine, theirs, lhs, rate, norm, ahead, behind):
    length = 2 * BLOCK
    slab = pl.BlockSpec((1, ROWS, length), lambda at: (at, 0, 0))
    return pl.pallas_call(
        tile_kernel,
        grid=(4,),
        in_specs=[
            pl.BlockSpec(memory_space=pltpu.SMEM),
            pl.BlockSpec(memory_space=pltpu.SMEM),
            whole(lhs.shape),
            whole(rate.shape),
            whole(norm.shape),
            slab,
            slab,
        ],
        out_specs=[
            pl.BlockSpec((1, 2, length, length), lambda at: (at, 0, 0, 0)),
            whole((8, length)),
        ],
        out_shape=[
            jax.ShapeDtypeStruct((4, 2, length, length), jnp.bfloat16),
            jax.ShapeDtypeStruct((8, length), jnp.float32),
        ],
        compiler_params=pltpu.CompilerParams(vmem_limit_bytes=VMEM_LIMIT),
        cost_estimate=pl.CostEstimate(
            flops=8 * 2 * ROWS * length * length, bytes_accessed=7 * 2**20, transcendentals=8 * length * length
        ),
    )(mine, theirs, lhs, rate, norm, ahead, behind)


def self_tiles(lhs, rate, norm, own):
    length = 2 * BLOCK
    return pl.pallas_call(
        self_kernel,
        out_shape=[
            jax.ShapeDtypeStruct((length, length), jnp.bfloat16),
            jax.ShapeDtypeStruct((8, length), jnp.float32),
        ],
        compiler_params=pltpu.CompilerParams(vmem_limit_bytes=VMEM_LIMIT),
        cost_estimate=pl.CostEstimate(
            flops=2 * ROWS * length * length, bytes_accessed=2**20, transcendentals=length * length
        ),
    )(lhs, rate, norm, own)


def gram_of(image):
    return lax.dot_general(
        image, image, TRANS_B, precision=lax.Precision.HIGHEST, preferred_element_type=jnp.float32
    )


def solved(gram, image):
    count = gram.shape[0]
    place = lax.broadcasted_iota(jnp.int32, (count, 1), 0)
    for k in range(count):
        inverse = 1.0 / jnp.sqrt(gram[k : k + 1, k : k + 1])
        gram_row = gram[k : k + 1, :] * inverse
        image_row = image[k : k + 1, :] * inverse
        column = jnp.where(place > k, gram[:, k : k + 1] * inverse, 0.0)
        gram = gram - column * gram_row
        image = jnp.where(place == k, image_row, image - column * image_row)
    return image


def weighted(vectors, tile):
    if vectors.dtype == jnp.bfloat16:
        return lax.dot_general(vectors, tile, TRANS_B, preferred_element_type=jnp.float32)
    count = vectors.shape[0]
    high = vectors.astype(jnp.bfloat16)
    low = (vectors - high.astype(jnp.float32)).astype(jnp.bfloat16)
    both = lax.dot_general(
        jnp.concatenate([high, low], 0), tile, TRANS_B, preferred_element_type=jnp.float32
    )
    return both[:count] + both[count:]


def sweep_kernel(own_ref, root_ref, self_ref, *refs):
    ahead_refs, behind_refs, tile_refs = refs[:3], refs[3:6], refs[6:9]
    image_ref, gram_ref, next_ref, total = refs[9:]
    at = pl.program_id(0)

    @pl.when(at == 0)
    def _():
        total[...] = weighted(own_ref[...], self_ref[...])

    part = None
    for ahead_ref, behind_ref, tile_ref in zip(ahead_refs, behind_refs, tile_refs):
        for side, data_ref in enumerate((ahead_ref, behind_ref)):
            term = weighted(data_ref[0], tile_ref[0, side])
            part = term if part is None else part + term
    total[...] += part

    @pl.when(at == 3)
    def _():
        image = root_ref[...] * total[...]
        image_ref[...] = image
        gram_ref[...] = gram_of(image)
        next_ref[...] = root_ref[...] * image


def sweep(own, root, self_tile, ahead, behind, tiles):
    vecs, length = own.shape
    slab = pl.BlockSpec((1, vecs, length), lambda at: (at, 0, 0))
    return pl.pallas_call(
        sweep_kernel,
        grid=(4,),
        in_specs=[whole(own.shape), whole(root.shape), whole(self_tile.shape)]
        + [slab] * 6
        + [pl.BlockSpec((1, 2, length, length), lambda at: (at, 0, 0, 0))] * 3,
        out_specs=[whole((vecs, length)), whole((vecs, vecs)), whole((vecs, length))],
        out_shape=[
            jax.ShapeDtypeStruct((vecs, length), jnp.float32),
            jax.ShapeDtypeStruct((vecs, vecs), jnp.float32),
            jax.ShapeDtypeStruct((vecs, length), jnp.float32),
        ],
        scratch_shapes=[pltpu.VMEM((vecs, length), jnp.float32)],
        compiler_params=pltpu.CompilerParams(vmem_limit_bytes=VMEM_LIMIT),
        cost_estimate=pl.CostEstimate(
            flops=25 * 2 * vecs * length * length, bytes_accessed=14 * 2**20, transcendentals=0
        ),
    )(own, root, self_tile, *[ahead[h] for h in (1, 2, 3)], *[behind[h] for h in (1, 2, 3)], *tiles)


def solve_gram_kernel(gram_ref, image_ref, solved_ref, next_ref):
    image = solved(gram_ref[...], image_ref[...])
    solved_ref[...] = image
    next_ref[...] = gram_of(image)


def solve_kernel(gram_ref, image_ref, solved_ref):
    solved_ref[...] = solved(gram_ref[...], image_ref[...])


def on_device(trajectories, kernel_scale, start_vectors, pair_list):
    length = trajectories.shape[1]
    vecs = start_vectors.shape[0]
    n_sub = lax.axis_size("sub")
    n_space = lax.axis_size("space")
    space_at = lax.axis_index("space")
    sub_at = lax.axis_index("sub")
    device = space_at * n_sub + sub_at

    row_blk = pair_list[:, 0] - device * 2
    col_dev = pair_list[:, 1] // 2
    hop = jnp.remainder(col_dev // n_sub - space_at, n_space)
    across = jnp.remainder(col_dev % n_sub - sub_at, n_sub)
    place = (((hop - 1) * 4 + across) * 2 + row_blk) * 2 + pair_list[:, 1] % 2
    place = jnp.where(hop > 0, place, -1)
    used = jnp.any(place[:, None] == jnp.arange(length, dtype=jnp.int32)[None, :], axis=0)
    payload = jnp.concatenate(
        [
            trajectories,
            kernel_scale[None, :],
            used.astype(jnp.bfloat16)[None, :],
            jnp.zeros((2, length), jnp.bfloat16),
        ],
        0,
    )

    group, ahead, behind = window_relayed(payload)

    rate = (LOG2E / kernel_scale.astype(jnp.float32))[:, None]
    norm = squares_of(trajectories).reshape(length, 1)
    lhs = jnp.concatenate(
        [trajectories.T * 2.0, jnp.zeros((length, ROWS - FEAT), jnp.bfloat16)], 1
    ).astype(jnp.bfloat16)

    mine = used[:48].astype(jnp.float32)

    def theirs_of(h):
        return behind[h][:, MASK_ROW, 16 * (h - 1) : 16 * h].astype(jnp.float32).reshape(64)

    self_tile, degree = self_tiles(lhs, rate, norm, payload)
    tiles = []
    for h in range(1, REACH + 1):
        tile, part = hop_tiles(mine[16 * (h - 1) : 16 * h], theirs_of(h), lhs, rate, norm, ahead[h], behind[h])
        tiles.append(tile)
        degree = degree + part
    root = lax.rsqrt(degree[:1])

    scaled = (root * start_vectors).astype(jnp.bfloat16)
    _, near_ahead, near_behind = window(scaled)
    image, gram, raw = sweep(scaled, root, self_tile, near_ahead, near_behind, tiles)

    gram = summed(gram)
    _, near_ahead, near_behind = window(raw)
    image, _, _ = sweep(raw, root, self_tile, near_ahead, near_behind, tiles)
    image, gram = pl.pallas_call(
        solve_gram_kernel,
        out_shape=[
            jax.ShapeDtypeStruct((vecs, length), jnp.float32),
            jax.ShapeDtypeStruct((vecs, vecs), jnp.float32),
        ],
        cost_estimate=pl.CostEstimate(flops=2**20, bytes_accessed=2**17, transcendentals=0),
    )(gram, image)
    gram = summed(gram)
    return pl.pallas_call(
        solve_kernel,
        out_shape=jax.ShapeDtypeStruct((vecs, length), jnp.float32),
        cost_estimate=pl.CostEstimate(flops=2**20, bytes_accessed=2**17, transcendentals=0),
    )(gram, image)


def solution(mesh):
    placed = (
        P(None, ("space", "sub")),
        P(("space", "sub")),
        P(None, ("space", "sub")),
        P(("space", "sub"), None),
    )
    return jax.shard_map(
        on_device, mesh=mesh, in_specs=placed, out_specs=P(None, ("space", "sub")), check_vma=False
    )
```

time: 484 us -> 253 us (0.52)
  blocking collectives: 184 us -> 0 us
  local copies, waits for them, and re-layouts: 63.5 us -> 2.3 us
  starting transfers between devices: 34.1 us -> 91.5 us
  Pallas kernels: 0 us -> 48.7 us
  other arithmetic: 41.6 us -> 8.04 us
  waiting for transfers between devices: 121 us -> 96.6 us
  matrix products: 21.1 us -> 0 us
  between operations: 14.2 us -> 0.41 us
    psum x2 -> x0, blocking collectives: 156 us -> none  [on_device(): lax.psum(jnp.dot(image, image.T, precision=lax.Precision.HIGHEST, preferr...]
    ppermute x18 -> x51, starting transfers between devices: 34 us -> 91.5 us  [shifted(): lax.ppermute(value, axis, [((at + steps) % count, at) for at in range(cou...]
    pallas_call x0 -> x8, Pallas kernels: none -> 48.7 us  [the longest x3 23.1 us: hop_tiles(): pl.pallas_call(tile_kernel, grid=(4,), in_specs=[pl.BlockSpec(memory_spac...]
    ppermute x18 -> x51, waiting for transfers between devices: 68.1 us -> 96.6 us  [shifted(): lax.ppermute(value, axis, [((at + steps) % count, at) for at in range(cou...]
    all_gather x1 -> x0, waiting for transfers between devices: 26.7 us -> none  [on_device(): whole = lax.all_gather(packed[None], 'sub', axis=0, tiled=True)]
    reduce_scatter x2 -> x0, waiting for transfers between devices: 26.2 us -> none  [return_far(): return lax.psum_scatter(returned, 'sub', scatter_dimension=0, tiled=True)[0]]
    all_gather x2 -> x0, blocking collectives: 19.7 us -> none  [nearby_vectors(): whole = lax.all_gather(scaled[None], 'sub', axis=0, tiled=True)]
    dot_general x15 -> x0, matrix products: 18.2 us -> none  [the longest x1 4.11 us: batch_similarity(): jnp.einsum('pfi,pfj->pij', row_coord, col_coord, preferred_element_type=j...]
  transfers between devices with their start and end apart: 21 -> 51, of which waited for: 10 -> 28; matrix products, arithmetic and copies ran while one was open for 13% -> 2% of each run, Pallas kernels for 0% -> 6%
where the time goes in v1:
time: 253 us; the launch traced here: 248 us
  waiting for transfers between devices  96.6 us (38%)
  starting transfers between devices  91.5 us (36%)
  Pallas kernels  48.7 us (19%)
  other arithmetic  8.04 us (3%)
    ppermute x51, waiting for transfers between devices, shifted(): lax.ppermute(value, axis, [((at + steps) % count, at) for at in range(cou...  96.6 us
    ppermute x51, starting transfers between devices, shifted(): lax.ppermute(value, axis, [((at + steps) % count, at) for at in range(cou...  91.5 us
    pallas_call x3, Pallas kernels, hop_tiles(): pl.pallas_call(tile_kernel, grid=(4,), in_specs=[pl.BlockSpec(memory_spac...  23.1 us
    pallas_call x2, Pallas kernels, sweep(): pl.pallas_call(sweep_kernel, grid=(4,), in_specs=[whole(own.shape), whole...  15.6 us
  transfers between devices with their start and end apart: 51, of which 28 were waited for; matrix products, arithmetic and copies ran while one was open for 2% of the time, Pallas kernels for 6%

profile of v1, /device:TPU:1, one launch (start us, length us, event | category | flops | bytes accessed | tf_op | source)
XLA Modules:
  0.0 247.6 jit_solution(10274860678913242551)
XLA Ops:
  2.8 3.6 %collective-permute-start = (bf16[304,512]{1,0:T(8,128)(2,1)S(1)}, bf16[304,512]{1,0:T(8,128)(2,1)S(1)}, u32[]{:S(2)}, u32[]{:S(2)}) collective-permute-start(bf16[304,512]{1,0:T(8,128)(2,1)S(1)} %maximum_maximum_fusion.own_ref), channel_id=1, source_target_pairs={{1,0},{2,1},{3,2},{0,3},{5,4},{6,5},{7,6},{4,7},{9,8},{10,9},{11,1... | collective-permute-start | bytes 933896 | tf_op jit(solution)/shard_map/ppermute | solution.py:24
  8.6 10.4 %collective-permute-done = bf16[304,512]{1,0:T(8,128)(2,1)S(1)} collective-permute-done((bf16[304,512]{1,0:T(8,128)(2,1)S(1)}, bf16[304,512]{1,0:T(8,128)(2,1)S(1)}, u32[]{:S(2)}, u32[]{:S(2)}) %collective-permute-start) | collective-permute-done | bytes 311328 | tf_op jit(solution)/shard_map/ppermute | solution.py:24
  19.0 4.9 %collective-permute-done.2 = bf16[304,512]{1,0:T(8,128)(2,1)S(1)} collective-permute-done((bf16[304,512]{1,0:T(8,128)(2,1)S(1)}, bf16[304,512]{1,0:T(8,128)(2,1)S(1)}, u32[]{:S(2)}, u32[]{:S(2)}) %collective-permute-start.2) | collective-permute-done | bytes 311328 | tf_op jit(solution)/shard_map/ppermute | solution.py:24
  26.3 6.6 %collective-permute-start.6 = (bf16[4,304,512]{2,1,0:T(8,128)(2,1)}, bf16[4,304,512]{2,1,0:T(8,128)(2,1)}, u32[]{:S(2)}, u32[]{:S(2)}) collective-permute-start(bf16[4,304,512]{2,1,0:T(8,128)(2,1)} %pad_maximum_fusion), channel_id=1, source_target_pairs={{8,0},{12,4},{16,8},{20,12},{24,16},{28,20},{32,24},{36,28},{40,32... | collective-permute-start | bytes 3735560 | tf_op jit(solution)/shard_map/ppermute | solution.py:24
  34.0 26.4 %collective-permute-done.5.behind_ref = bf16[4,304,512]{2,1,0:T(8,128)(2,1)S(1)} collective-permute-done((bf16[4,304,512]{2,1,0:T(8,128)(2,1)}, bf16[4,304,512]{2,1,0:T(8,128)(2,1)S(1)}, u32[]{:S(2)}, u32[]{:S(2)}) %collective-permute-start.5) | collective-permute-done | bytes 1245216 | tf_op jit(solution)/shard_map/ppermute | solution.py:24
  60.4 1.6 collective-permute-start.8
  63.4 3.8 %collective-permute-done.3.behind_ref = bf16[4,304,512]{2,1,0:T(8,128)(2,1)} collective-permute-done((bf16[4,304,512]{2,1,0:T(8,128)(2,1)}, bf16[4,304,512]{2,1,0:T(8,128)(2,1)}, u32[]{:S(2)}, u32[]{:S(2)}) %collective-permute-start.3) | collective-permute-done | bytes 1245216 | tf_op jit(solution)/shard_map/ppermute | solution.py:24
  68.1 7.5 %shard_map.48 = (bf16[4,2,512,512]{3,2,1,0:T(8,128)(2,1)}, f32[8,512]{1,0:T(8,128)S(1)}) custom-call(f32[16]{0:T(128)S(1)} %get-tuple-element.33.mine_ref, f32[64]{0:T(128)S(1)} %reshape.23.theirs_ref, bf16[512,304]{1,0:T(8,128)(2,1)S(1)} %concatenate.6.lhs_ref, f32[512,1]{1,0:T(8,128)S(1)} %copy.26.rate_ref, f32[512,1]{1,0:T(8,128)S(1)} %copy.27.norm_ref, ...), custom_call_target="tpu_custom_call" | custom-call | flops 1275068416 | bytes 7340032 | tf_op jit(solution)/shard_map/pallas_call | solution.py:123
  75.7 7.7 %shard_map.47 = (bf16[4,2,512,512]{3,2,1,0:T(8,128)(2,1)}, f32[8,512]{1,0:T(8,128)S(1)}) custom-call(f32[16]{0:T(128)S(1)} %get-tuple-element.31.mine_ref, f32[64]{0:T(128)S(1)} %reshape.22.theirs_ref, bf16[512,304]{1,0:T(8,128)(2,1)S(1)} %concatenate.6.lhs_ref, f32[512,1]{1,0:T(8,128)S(1)} %copy.26.rate_ref, f32[512,1]{1,0:T(8,128)S(1)} %copy.27.norm_ref, ...), custom_call_target="tpu_custom_call" | custom-call | flops 1275068416 | bytes 7340032 | tf_op jit(solution)/shard_map/pallas_call | solution.py:123
  84.3 7.9 %shard_map.49 = (bf16[4,2,512,512]{3,2,1,0:T(8,128)(2,1)}, f32[8,512]{1,0:T(8,128)S(1)}) custom-call(f32[16]{0:T(128)S(1)} %get-tuple-element.32.mine_ref, f32[64]{0:T(128)S(1)} %reshape.24.theirs_ref, bf16[512,304]{1,0:T(8,128)(2,1)S(1)} %concatenate.6.lhs_ref, f32[512,1]{1,0:T(8,128)S(1)} %copy.26.rate_ref, f32[512,1]{1,0:T(8,128)S(1)} %copy.27.norm_ref, ...), custom_call_target="tpu_custom_call" | custom-call | flops 1275068416 | bytes 7340032 | tf_op jit(solution)/shard_map/pallas_call | solution.py:123
  94.0 1.3 collective-permute-done.9
  95.3 1.6 collective-permute-done.10
  97.7 9.2 %collective-permute-start.12 = (bf16[4,32,512]{2,1,0:T(8,128)(2,1)S(1)}, bf16[4,32,512]{2,1,0:T(8,128)(2,1)S(1)}, u32[]{:S(2)}, u32[]{:S(2)}) collective-permute-start(bf16[4,32,512]{2,1,0:T(8,128)(2,1)S(1)} %pad_maximum_fusion.2), channel_id=1, source_target_pairs={{4,0},{8,4},{12,8},{16,12},{20,16},{24,20},{28,24},{32,28},{36,32}... | collective-permute-start | bytes 393224 | tf_op jit(solution)/shard_map/ppermute | solution.py:24
  106.9 1.5 collective-permute-start.13
  109.8 1.5 collective-permute-start.16
  111.3 1.2 collective-permute-start.17
  112.5 3.1 %collective-permute-done.14.refs_2_ = bf16[4,32,512]{2,1,0:T(8,128)(2,1)S(1)} collective-permute-done((bf16[4,32,512]{2,1,0:T(8,128)(2,1)S(1)}, bf16[4,32,512]{2,1,0:T(8,128)(2,1)S(1)}, u32[]{:S(2)}, u32[]{:S(2)}) %collective-permute-start.14) | collective-permute-done | bytes 131104 | tf_op jit(solution)/shard_map/ppermute | solution.py:24
  115.6 5.6 %collective-permute-done.16.refs_4_ = bf16[4,32,512]{2,1,0:T(8,128)(2,1)S(1)} collective-permute-done((bf16[4,32,512]{2,1,0:T(8,128)(2,1)S(1)}, bf16[4,32,512]{2,1,0:T(8,128)(2,1)S(1)}, u32[]{:S(2)}, u32[]{:S(2)}) %collective-permute-start.16) | collective-permute-done | bytes 131104 | tf_op jit(solution)/shard_map/ppermute | solution.py:24
  122.4 7.4 %shard_map.50 = (f32[32,512]{1,0:T(8,128)}, f32[32,32]{1,0:T(8,128)S(1)}, f32[32,512]{1,0:T(8,128)S(1)}) custom-call(bf16[32,512]{1,0:T(8,128)(2,1)S(1)} %multiply_convert_fusion.own_ref, f32[1,512]{1,0:T(1,128)S(1)} %fusion.1.root_ref, bf16[512,512]{1,0:T(8,128)(2,1)S(1)} %get-tuple-element.22.self_ref, ...), custom_call_target="tpu_custom_call" | custom-call | flops 419430400 | bytes 14680064 | tf_op jit(solution)/shard_map/pallas_call | solution.py:223
  129.7 1.7 collective-permute-start.18
  132.1 2.7 %collective-permute-start.30 = (f32[32,512]{1,0:T(8,128)S(1)}, f32[32,512]{1,0:T(8,128)S(1)}, u32[]{:S(2)}, u32[]{:S(2)}) collective-permute-start(f32[32,512]{1,0:T(8,128)S(1)} %get-tuple-element.27.own_ref), channel_id=1, source_target_pairs={{1,0},{2,1},{3,2},{0,3},{5,4},{6,5},{7,6},{4,7},{9,8},{10,9},{11,1... | collective-permute-start | bytes 196616 | tf_op jit(solution)/shard_map/ppermute | solution.py:24
  138.0 9.8 %collective-permute-start.23 = (f32[32,32]{1,0:T(8,128)S(1)}, f32[32,32]{1,0:T(8,128)S(1)}, u32[]{:S(2)}, u32[]{:S(2)}) collective-permute-start(f32[32,32]{1,0:T(8,128)S(1)} %add_add_fusion.7), channel_id=1, source_target_pairs={{12,0},{16,4},{20,8},{24,12},{28,16},{32,20},{36,24},{40,28},{44,3... | collective-permute-start | bytes 12296 | tf_op jit(solution)/shard_map/ppermute | solution.py:24
  147.9 2.9 %collective-permute-start.33 = (f32[4,32,512]{2,1,0:T(8,128)S(1)}, f32[4,32,512]{2,1,0:T(8,128)S(1)}, u32[]{:S(2)}, u32[]{:S(2)}) collective-permute-start(f32[4,32,512]{2,1,0:T(8,128)S(1)} %pad_maximum_fusion.1), channel_id=1, source_target_pairs={{4,0},{8,4},{12,8},{16,12},{20,16},{24,20},{28,24},{32,28},{36,32}... | collective-permute-start | bytes 786440 | tf_op jit(solution)/shard_map/ppermute | solution.py:24
  151.6 5.5 %collective-permute-start.24 = (f32[32,32]{1,0:T(8,128)S(1)}, f32[32,32]{1,0:T(8,128)S(1)}, u32[]{:S(2)}, u32[]{:S(2)}) collective-permute-start(f32[32,32]{1,0:T(8,128)S(1)} %add_add_fusion.6), channel_id=1, source_target_pairs={{16,0},{20,4},{24,8},{28,12},{32,16},{36,20},{40,24},{44,28},{48,3... | collective-permute-start | bytes 12296 | tf_op jit(solution)/shard_map/ppermute | solution.py:24
  158.0 2.1 collective-permute-done.25
  160.1 2.1 collective-permute-done.26
  162.2 4.1 %collective-permute-start.28 = (f32[32,32]{1,0:T(8,128)S(1)}, f32[32,32]{1,0:T(8,128)S(1)}, u32[]{:S(2)}, u32[]{:S(2)}) collective-permute-start(f32[32,32]{1,0:T(8,128)S(1)} %add_add_fusion.5), channel_id=1, source_target_pairs={{128,0},{132,4},{136,8},{140,12},{144,16},{148,20},{152,24},{156,2... | collective-permute-start | bytes 12296 | tf_op jit(solution)/shard_map/ppermute | solution.py:24
  166.3 1.4 collective-permute-start.34
  167.8 2.5 %collective-permute-start.35 = (f32[4,32,512]{2,1,0:T(8,128)S(1)}, f32[4,32,512]{2,1,0:T(8,128)S(1)}, u32[]{:S(2)}, u32[]{:S(2)}) collective-permute-start(f32[4,32,512]{2,1,0:T(8,128)S(1)} %pad_maximum_fusion.1), channel_id=1, source_target_pairs={{12,0},{16,4},{20,8},{24,12},{28,16},{32,20},{36,24},{40,28},{44,3... | collective-permute-start | bytes 786440 | tf_op jit(solution)/shard_map/ppermute | solution.py:24
  171.1 1.3 collective-permute-start.37
  172.4 3.2 %collective-permute-start.38 = (f32[4,32,512]{2,1,0:T(8,128)S(1)}, f32[4,32,512]{2,1,0:T(8,128)S(1)}, u32[]{:S(2)}, u32[]{:S(2)}) collective-permute-start(f32[4,32,512]{2,1,0:T(8,128)S(1)} %pad_maximum_fusion.1), channel_id=1, source_target_pairs={{244,0},{248,4},{252,8},{0,12},{4,16},{8,20},{12,24},{16,28},{20,3... | collective-permute-start | bytes 786440 | tf_op jit(solution)/shard_map/ppermute | solution.py:24
  176.8 2.3 collective-permute-done.35.refs_2_
  179.1 9.0 %collective-permute-done.37.refs_4_ = f32[4,32,512]{2,1,0:T(8,128)S(1)} collective-permute-done((f32[4,32,512]{2,1,0:T(8,128)S(1)}, f32[4,32,512]{2,1,0:T(8,128)S(1)}, u32[]{:S(2)}, u32[]{:S(2)}) %collective-permute-start.37) | collective-permute-done | bytes 262176 | tf_op jit(solution)/shard_map/ppermute | solution.py:24
  188.1 4.5 %collective-permute-done.38.refs_5_ = f32[4,32,512]{2,1,0:T(8,128)S(1)} collective-permute-done((f32[4,32,512]{2,1,0:T(8,128)S(1)}, f32[4,32,512]{2,1,0:T(8,128)S(1)}, u32[]{:S(2)}, u32[]{:S(2)}) %collective-permute-start.38) | collective-permute-done | bytes 262176 | tf_op jit(solution)/shard_map/ppermute | solution.py:24
  192.6 8.2 %shard_map.51 = (f32[32,512]{1,0:T(8,128)S(1)}, f32[32,32]{1,0:T(8,128)}, f32[32,512]{1,0:T(8,128)}) custom-call(f32[32,512]{1,0:T(8,128)S(1)} %get-tuple-element.27.own_ref, f32[1,512]{1,0:T(1,128)S(1)} %fusion.1.root_ref, bf16[512,512]{1,0:T(8,128)(2,1)S(1)} %get-tuple-element.22.self_ref, f32[4,32,512]{2,1,0:T(8,128)S(1)} %collective-permute-done.33.refs_0_, ...), custom_call_target="tpu_custom_call" | custom-call | flops 419430400 | bytes 14680064 | tf_op jit(solution)/shard_map/pallas_call | solution.py:223
  201.5 4.7 %shard_map.52 = (f32[32,512]{1,0:T(8,128)}, f32[32,32]{1,0:T(8,128)}) custom-call(f32[32,32]{1,0:T(8,128)} %add_add_fusion.4.gram_ref, f32[32,512]{1,0:T(8,128)} %copy-done.1), custom_call_target="tpu_custom_call" | custom-call | flops 1048576 | bytes 131072 | tf_op jit(solution)/shard_map/pallas_call | solution.py:307
  206.2 2.6 %collective-permute-start.39 = (f32[32,32]{1,0:T(8,128)}, f32[32,32]{1,0:T(8,128)S(1)}, u32[]{:S(2)}, u32[]{:S(2)}) collective-permute-start(f32[32,32]{1,0:T(8,128)} %get-tuple-element.29), channel_id=1, source_target_pairs={{1,0},{2,1},{3,2},{0,3},{5,4},{6,5},{7,6},{4,7},{9,8},{10,9},{11,1... | collective-permute-start | bytes 12296 | tf_op jit(solution)/shard_map/ppermute | solution.py:24
  209.8 3.2 %collective-permute-done.40 = f32[32,32]{1,0:T(8,128)S(1)} collective-permute-done((f32[32,32]{1,0:T(8,128)}, f32[32,32]{1,0:T(8,128)S(1)}, u32[]{:S(2)}, u32[]{:S(2)}) %collective-permute-start.40) | collective-permute-done | bytes 4128 | tf_op jit(solution)/shard_map/ppermute | solution.py:24
  214.3 1.7 collective-permute-start.43
  216.1 3.3 %collective-permute-start.44 = (f32[32,32]{1,0:T(8,128)S(1)}, f32[32,32]{1,0:T(8,128)S(1)}, u32[]{:S(2)}, u32[]{:S(2)}) collective-permute-start(f32[32,32]{1,0:T(8,128)S(1)} %add_add_fusion.3), channel_id=1, source_target_pairs={{12,0},{16,4},{20,8},{24,12},{28,16},{32,20},{36,24},{40,28},{44,3... | collective-permute-start | bytes 12296 | tf_op jit(solution)/shard_map/ppermute | solution.py:24
  219.6 1.7 collective-permute-done.44
  221.3 4.9 %collective-permute-start.45 = (f32[32,32]{1,0:T(8,128)S(1)}, f32[32,32]{1,0:T(8,128)S(1)}, u32[]{:S(2)}, u32[]{:S(2)}) collective-permute-start(f32[32,32]{1,0:T(8,128)S(1)} %add_add_fusion.2), channel_id=1, source_target_pairs={{16,0},{20,4},{24,8},{28,12},{32,16},{36,20},{40,24},{44,28},{48,3... | collective-permute-start | bytes 12296 | tf_op jit(solution)/shard_map/ppermute | solution.py:24
  227.1 1.8 collective-permute-done.46
  228.9 2.7 %collective-permute-done.47 = f32[32,32]{1,0:T(8,128)S(1)} collective-permute-done((f32[32,32]{1,0:T(8,128)S(1)}, f32[32,32]{1,0:T(8,128)S(1)}, u32[]{:S(2)}, u32[]{:S(2)}) %collective-permute-start.47) | collective-permute-done | bytes 4128 | tf_op jit(solution)/shard_map/ppermute | solution.py:24
  231.6 4.0 %collective-permute-start.48 = (f32[32,32]{1,0:T(8,128)S(1)}, f32[32,32]{1,0:T(8,128)S(1)}, u32[]{:S(2)}, u32[]{:S(2)}) collective-permute-start(f32[32,32]{1,0:T(8,128)S(1)} %add_add_fusion.1), channel_id=1, source_target_pairs={{64,0},{68,4},{72,8},{76,12},{80,16},{84,20},{88,24},{92,28},{96,3... | collective-permute-start | bytes 12296 | tf_op jit(solution)/shard_map/ppermute | solution.py:24
  236.1 2.2 collective-permute-start.50
  238.2 4.0 %collective-permute-done.49 = f32[32,32]{1,0:T(8,128)S(1)} collective-permute-done((f32[32,32]{1,0:T(8,128)S(1)}, f32[32,32]{1,0:T(8,128)S(1)}, u32[]{:S(2)}, u32[]{:S(2)}) %collective-permute-start.49) | collective-permute-done | bytes 4128 | tf_op jit(solution)/shard_map/ppermute | solution.py:24
  242.9 4.5 %shard_map.53 = f32[32,512]{1,0:T(8,128)} custom-call(f32[32,32]{1,0:T(8,128)} %add_add_fusion.gram_ref, f32[32,512]{1,0:T(8,128)} %get-tuple-element.30.image_ref), custom_call_target="tpu_custom_call" | custom-call | flops 1048576 | bytes 131072 | tf_op jit(solution)/shard_map/pallas_call | solution.py:316
  (110 shorter events, 29.7 us)
Async XLA Ops:
  2.8 16.2 %collective-permute-start = (bf16[304,512]{1,0:T(8,128)(2,1)S(1)}, bf16[304,512]{1,0:T(8,128)(2,1)S(1)}, u32[]{:S(2)}, u32[]{:S(2)}) collective-permute-start(bf16[304,512]{1,0:T(8,128)(2,1)S(1)} %maximum_maximum_fusion.own_ref), channel_id=1, source_target_pairs={{1,0},{2,1},{3,2},{0,3},{5,4},{6,5},{7,6},{4,7},{9,8},{10,9},{11,1... | collective-permute-start | bytes 933896 | tf_op jit(solution)/shard_map/ppermute | solution.py:24
  6.4 12.6 %collective-permute-start.1 = (bf16[304,512]{1,0:T(8,128)(2,1)S(1)}, bf16[304,512]{1,0:T(8,128)(2,1)S(1)}, u32[]{:S(2)}, u32[]{:S(2)}) collective-permute-start(bf16[304,512]{1,0:T(8,128)(2,1)S(1)} %maximum_maximum_fusion.own_ref), channel_id=1, source_target_pairs={{2,0},{3,1},{0,2},{1,3},{6,4},{7,5},{4,6},{5,7},{10,8},{11,9},{8,1... | collective-permute-start | bytes 933896 | tf_op jit(solution)/shard_map/ppermute | solution.py:24
  6.8 17.1 %collective-permute-start.2 = (bf16[304,512]{1,0:T(8,128)(2,1)S(1)}, bf16[304,512]{1,0:T(8,128)(2,1)S(1)}, u32[]{:S(2)}, u32[]{:S(2)}) collective-permute-start(bf16[304,512]{1,0:T(8,128)(2,1)S(1)} %maximum_maximum_fusion.own_ref), channel_id=1, source_target_pairs={{3,0},{0,1},{1,2},{2,3},{7,4},{4,5},{5,6},{6,7},{11,8},{8,9},{9,10... | collective-permute-start | bytes 933896 | tf_op jit(solution)/shard_map/ppermute | solution.py:24
  25.1 35.3 %collective-permute-start.5 = (bf16[4,304,512]{2,1,0:T(8,128)(2,1)}, bf16[4,304,512]{2,1,0:T(8,128)(2,1)S(1)}, u32[]{:S(2)}, u32[]{:S(2)}) collective-permute-start(bf16[4,304,512]{2,1,0:T(8,128)(2,1)} %pad_maximum_fusion), channel_id=1, source_target_pairs={{248,0},{252,4},{0,8},{4,12},{8,16},{12,20},{16,24},{20,28},{24,32... | collective-permute-start | bytes 3735560 | tf_op jit(solution)/shard_map/ppermute | solution.py:24
  26.3 34.1 %collective-permute-start.6 = (bf16[4,304,512]{2,1,0:T(8,128)(2,1)}, bf16[4,304,512]{2,1,0:T(8,128)(2,1)}, u32[]{:S(2)}, u32[]{:S(2)}) collective-permute-start(bf16[4,304,512]{2,1,0:T(8,128)(2,1)} %pad_maximum_fusion), channel_id=1, source_target_pairs={{8,0},{12,4},{16,8},{20,12},{24,16},{28,20},{32,24},{36,28},{40,32... | collective-permute-start | bytes 3735560 | tf_op jit(solution)/shard_map/ppermute | solution.py:24
  32.8 34.3 %collective-permute-start.3 = (bf16[4,304,512]{2,1,0:T(8,128)(2,1)}, bf16[4,304,512]{2,1,0:T(8,128)(2,1)}, u32[]{:S(2)}, u32[]{:S(2)}) collective-permute-start(bf16[4,304,512]{2,1,0:T(8,128)(2,1)} %pad_maximum_fusion), channel_id=1, source_target_pairs={{252,0},{0,4},{4,8},{8,12},{12,16},{16,20},{20,24},{24,28},{28,32}... | collective-permute-start | bytes 3735560 | tf_op jit(solution)/shard_map/ppermute | solution.py:24
  33.1 42.6 %collective-permute-start.4 = (bf16[4,304,512]{2,1,0:T(8,128)(2,1)}, bf16[4,304,512]{2,1,0:T(8,128)(2,1)}, u32[]{:S(2)}, u32[]{:S(2)}) collective-permute-start(bf16[4,304,512]{2,1,0:T(8,128)(2,1)} %pad_maximum_fusion), channel_id=1, source_target_pairs={{4,0},{8,4},{12,8},{16,12},{20,16},{24,20},{28,24},{32,28},{36,32}... | collective-permute-start | bytes 3735560 | tf_op jit(solution)/shard_map/ppermute | solution.py:24
  60.3 23.0 %collective-permute-start.7 = (bf16[4,304,512]{2,1,0:T(8,128)(2,1)S(1)}, bf16[4,304,512]{2,1,0:T(8,128)(2,1)}, u32[]{:S(2)}, u32[]{:S(2)}) collective-permute-start(bf16[4,304,512]{2,1,0:T(8,128)(2,1)S(1)} %collective-permute-done.5.behind_ref), channel_id=1, source_target_pairs={{252,0},{0,4},{4,8},{8,12},{12,16},{16,20},{20,24},{24,28},{28,32}... | collective-permute-start | bytes 3735560 | tf_op jit(solution)/shard_map/ppermute | solution.py:24
  60.4 23.9 %collective-permute-start.8 = (bf16[4,304,512]{2,1,0:T(8,128)(2,1)}, bf16[4,304,512]{2,1,0:T(8,128)(2,1)}, u32[]{:S(2)}, u32[]{:S(2)}) collective-permute-start(bf16[4,304,512]{2,1,0:T(8,128)(2,1)} %collective-permute-done.6.ahead_ref), channel_id=1, source_target_pairs={{4,0},{8,4},{12,8},{16,12},{20,16},{24,20},{28,24},{32,28},{36,32}... | collective-permute-start | bytes 3735560 | tf_op jit(solution)/shard_map/ppermute | solution.py:24
  92.5 4.4 %collective-permute-start.10 = (bf16[32,512]{1,0:T(8,128)(2,1)S(1)}, bf16[32,512]{1,0:T(8,128)(2,1)S(1)}, u32[]{:S(2)}, u32[]{:S(2)}) collective-permute-start(bf16[32,512]{1,0:T(8,128)(2,1)S(1)} %multiply_convert_fusion.own_ref), channel_id=1, source_target_pairs={{2,0},{3,1},{0,2},{1,3},{6,4},{7,5},{4,6},{5,7},{10,8},{11,9},{8,1... | collective-permute-start | bytes 98312 | tf_op jit(solution)/shard_map/ppermute | solution.py:24
  92.9 4.7 %collective-permute-start.11 = (bf16[32,512]{1,0:T(8,128)(2,1)S(1)}, bf16[32,512]{1,0:T(8,128)(2,1)S(1)}, u32[]{:S(2)}, u32[]{:S(2)}) collective-permute-start(bf16[32,512]{1,0:T(8,128)(2,1)S(1)} %multiply_convert_fusion.own_ref), channel_id=1, source_target_pairs={{3,0},{0,1},{1,2},{2,3},{7,4},{4,5},{5,6},{6,7},{11,8},{8,9},{9,10... | collective-permute-start | bytes 98312 | tf_op jit(solution)/shard_map/ppermute | solution.py:24
  97.7 13.6 %collective-permute-start.12 = (bf16[4,32,512]{2,1,0:T(8,128)(2,1)S(1)}, bf16[4,32,512]{2,1,0:T(8,128)(2,1)S(1)}, u32[]{:S(2)}, u32[]{:S(2)}) collective-permute-start(bf16[4,32,512]{2,1,0:T(8,128)(2,1)S(1)} %pad_maximum_fusion.2), channel_id=1, source_target_pairs={{4,0},{8,4},{12,8},{16,12},{20,16},{24,20},{28,24},{32,28},{36,32}... | collective-permute-start | bytes 393224 | tf_op jit(solution)/shard_map/ppermute | solution.py:24
  106.9 5.7 %collective-permute-start.13 = (bf16[4,32,512]{2,1,0:T(8,128)(2,1)S(1)}, bf16[4,32,512]{2,1,0:T(8,128)(2,1)S(1)}, u32[]{:S(2)}, u32[]{:S(2)}) collective-permute-start(bf16[4,32,512]{2,1,0:T(8,128)(2,1)S(1)} %pad_maximum_fusion.2), channel_id=1, source_target_pairs={{8,0},{12,4},{16,8},{20,12},{24,16},{28,20},{32,24},{36,28},{40,32... | collective-permute-start | bytes 393224 | tf_op jit(solution)/shard_map/ppermute | solution.py:24
  108.4 7.3 %collective-permute-start.14 = (bf16[4,32,512]{2,1,0:T(8,128)(2,1)S(1)}, bf16[4,32,512]{2,1,0:T(8,128)(2,1)S(1)}, u32[]{:S(2)}, u32[]{:S(2)}) collective-permute-start(bf16[4,32,512]{2,1,0:T(8,128)(2,1)S(1)} %pad_maximum_fusion.2), channel_id=1, source_target_pairs={{12,0},{16,4},{20,8},{24,12},{28,16},{32,20},{36,24},{40,28},{44,3... | collective-permute-start | bytes 393224 | tf_op jit(solution)/shard_map/ppermute | solution.py:24
  109.1 6.5 %collective-permute-start.15 = (bf16[4,32,512]{2,1,0:T(8,128)(2,1)S(1)}, bf16[4,32,512]{2,1,0:T(8,128)(2,1)S(1)}, u32[]{:S(2)}, u32[]{:S(2)}) collective-permute-start(bf16[4,32,512]{2,1,0:T(8,128)(2,1)S(1)} %pad_maximum_fusion.2), channel_id=1, source_target_pairs={{252,0},{0,4},{4,8},{8,12},{12,16},{16,20},{20,24},{24,28},{28,32}... | collective-permute-start | bytes 393224 | tf_op jit(solution)/shard_map/ppermute | solution.py:24
  109.8 11.4 %collective-permute-start.16 = (bf16[4,32,512]{2,1,0:T(8,128)(2,1)S(1)}, bf16[4,32,512]{2,1,0:T(8,128)(2,1)S(1)}, u32[]{:S(2)}, u32[]{:S(2)}) collective-permute-start(bf16[4,32,512]{2,1,0:T(8,128)(2,1)S(1)} %pad_maximum_fusion.2), channel_id=1, source_target_pairs={{248,0},{252,4},{0,8},{4,12},{8,16},{12,20},{16,24},{20,28},{24,32... | collective-permute-start | bytes 393224 | tf_op jit(solution)/shard_map/ppermute | solution.py:24
  111.3 11.1 %collective-permute-start.17 = (bf16[4,32,512]{2,1,0:T(8,128)(2,1)S(1)}, bf16[4,32,512]{2,1,0:T(8,128)(2,1)S(1)}, u32[]{:S(2)}, u32[]{:S(2)}) collective-permute-start(bf16[4,32,512]{2,1,0:T(8,128)(2,1)S(1)} %pad_maximum_fusion.2), channel_id=1, source_target_pairs={{244,0},{248,4},{252,8},{0,12},{4,16},{8,20},{12,24},{16,28},{20,3... | collective-permute-start | bytes 393224 | tf_op jit(solution)/shard_map/ppermute | solution.py:24
  129.7 6.2 %collective-permute-start.18 = (f32[32,32]{1,0:T(8,128)S(1)}, f32[32,32]{1,0:T(8,128)S(1)}, u32[]{:S(2)}, u32[]{:S(2)}) collective-permute-start(f32[32,32]{1,0:T(8,128)S(1)} %get-tuple-element.26), channel_id=1, source_target_pairs={{1,0},{2,1},{3,2},{0,3},{5,4},{6,5},{7,6},{4,7},{9,8},{10,9},{11,1... | collective-permute-start | bytes 12296 | tf_op jit(solution)/shard_map/ppermute | solution.py:24
  131.5 4.4 %collective-permute-start.19 = (f32[32,32]{1,0:T(8,128)S(1)}, f32[32,32]{1,0:T(8,128)S(1)}, u32[]{:S(2)}, u32[]{:S(2)}) collective-permute-start(f32[32,32]{1,0:T(8,128)S(1)} %get-tuple-element.26), channel_id=1, source_target_pairs={{2,0},{3,1},{0,2},{1,3},{6,4},{7,5},{4,6},{5,7},{10,8},{11,9},{8,1... | collective-permute-start | bytes 12296 | tf_op jit(solution)/shard_map/ppermute | solution.py:24
  132.1 3.8 %collective-permute-start.20 = (f32[32,32]{1,0:T(8,128)S(1)}, f32[32,32]{1,0:T(8,128)S(1)}, u32[]{:S(2)}, u32[]{:S(2)}) collective-permute-start(f32[32,32]{1,0:T(8,128)S(1)} %get-tuple-element.26), channel_id=1, source_target_pairs={{3,0},{0,1},{1,2},{2,3},{7,4},{4,5},{5,6},{6,7},{11,8},{8,9},{9,10... | collective-permute-start | bytes 12296 | tf_op jit(solution)/shard_map/ppermute | solution.py:24
  132.1 5.9 %collective-permute-start.30 = (f32[32,512]{1,0:T(8,128)S(1)}, f32[32,512]{1,0:T(8,128)S(1)}, u32[]{:S(2)}, u32[]{:S(2)}) collective-permute-start(f32[32,512]{1,0:T(8,128)S(1)} %get-tuple-element.27.own_ref), channel_id=1, source_target_pairs={{1,0},{2,1},{3,2},{0,3},{5,4},{6,5},{7,6},{4,7},{9,8},{10,9},{11,1... | collective-permute-start | bytes 196616 | tf_op jit(solution)/shard_map/ppermute | solution.py:24
  134.8 13.0 %collective-permute-start.31 = (f32[32,512]{1,0:T(8,128)S(1)}, f32[32,512]{1,0:T(8,128)S(1)}, u32[]{:S(2)}, u32[]{:S(2)}) collective-permute-start(f32[32,512]{1,0:T(8,128)S(1)} %get-tuple-element.27.own_ref), channel_id=1, source_target_pairs={{2,0},{3,1},{0,2},{1,3},{6,4},{7,5},{4,6},{5,7},{10,8},{11,9},{8,1... | collective-permute-start | bytes 196616 | tf_op jit(solution)/shard_map/ppermute | solution.py:24
  135.9 11.9 %collective-permute-start.32 = (f32[32,512]{1,0:T(8,128)S(1)}, f32[32,512]{1,0:T(8,128)S(1)}, u32[]{:S(2)}, u32[]{:S(2)}) collective-permute-start(f32[32,512]{1,0:T(8,128)S(1)} %get-tuple-element.27.own_ref), channel_id=1, source_target_pairs={{3,0},{0,1},{1,2},{2,3},{7,4},{4,5},{5,6},{6,7},{11,8},{8,9},{9,10... | collective-permute-start | bytes 196616 | tf_op jit(solution)/shard_map/ppermute | solution.py:24
  136.0 14.8 %collective-permute-start.21 = (f32[32,32]{1,0:T(8,128)S(1)}, f32[32,32]{1,0:T(8,128)S(1)}, u32[]{:S(2)}, u32[]{:S(2)}) collective-permute-start(f32[32,32]{1,0:T(8,128)S(1)} %add_add_fusion.7), channel_id=1, source_target_pairs={{4,0},{8,4},{12,8},{16,12},{20,16},{24,20},{28,24},{32,28},{36,32}... | collective-permute-start | bytes 12296 | tf_op jit(solution)/shard_map/ppermute | solution.py:24
  136.4 14.4 %collective-permute-start.22 = (f32[32,32]{1,0:T(8,128)S(1)}, f32[32,32]{1,0:T(8,128)S(1)}, u32[]{:S(2)}, u32[]{:S(2)}) collective-permute-start(f32[32,32]{1,0:T(8,128)S(1)} %add_add_fusion.7), channel_id=1, source_target_pairs={{8,0},{12,4},{16,8},{20,12},{24,16},{28,20},{32,24},{36,28},{40,32... | collective-permute-start | bytes 12296 | tf_op jit(solution)/shard_map/ppermute | solution.py:24
  138.0 13.6 %collective-permute-start.23 = (f32[32,32]{1,0:T(8,128)S(1)}, f32[32,32]{1,0:T(8,128)S(1)}, u32[]{:S(2)}, u32[]{:S(2)}) collective-permute-start(f32[32,32]{1,0:T(8,128)S(1)} %add_add_fusion.7), channel_id=1, source_target_pairs={{12,0},{16,4},{20,8},{24,12},{28,16},{32,20},{36,24},{40,28},{44,3... | collective-permute-start | bytes 12296 | tf_op jit(solution)/shard_map/ppermute | solution.py:24
  147.9 24.6 %collective-permute-start.33 = (f32[4,32,512]{2,1,0:T(8,128)S(1)}, f32[4,32,512]{2,1,0:T(8,128)S(1)}, u32[]{:S(2)}, u32[]{:S(2)}) collective-permute-start(f32[4,32,512]{2,1,0:T(8,128)S(1)} %pad_maximum_fusion.1), channel_id=1, source_target_pairs={{4,0},{8,4},{12,8},{16,12},{20,16},{24,20},{28,24},{32,28},{36,32}... | collective-permute-start | bytes 786440 | tf_op jit(solution)/shard_map/ppermute | solution.py:24
  151.6 6.4 %collective-permute-start.24 = (f32[32,32]{1,0:T(8,128)S(1)}, f32[32,32]{1,0:T(8,128)S(1)}, u32[]{:S(2)}, u32[]{:S(2)}) collective-permute-start(f32[32,32]{1,0:T(8,128)S(1)} %add_add_fusion.6), channel_id=1, source_target_pairs={{16,0},{20,4},{24,8},{28,12},{32,16},{36,20},{40,24},{44,28},{48,3... | collective-permute-start | bytes 12296 | tf_op jit(solution)/shard_map/ppermute | solution.py:24
  157.2 5.0 %collective-permute-start.26 = (f32[32,32]{1,0:T(8,128)S(1)}, f32[32,32]{1,0:T(8,128)S(1)}, u32[]{:S(2)}, u32[]{:S(2)}) collective-permute-start(f32[32,32]{1,0:T(8,128)S(1)} %add_add_fusion.6), channel_id=1, source_target_pairs={{48,0},{52,4},{56,8},{60,12},{64,16},{68,20},{72,24},{76,28},{80,3... | collective-permute-start | bytes 12296 | tf_op jit(solution)/shard_map/ppermute | solution.py:24
  162.2 5.6 %collective-permute-start.27 = (f32[32,32]{1,0:T(8,128)S(1)}, f32[32,32]{1,0:T(8,128)S(1)}, u32[]{:S(2)}, u32[]{:S(2)}) collective-permute-start(f32[32,32]{1,0:T(8,128)S(1)} %add_add_fusion.5), channel_id=1, source_target_pairs={{64,0},{68,4},{72,8},{76,12},{80,16},{84,20},{88,24},{92,28},{96,3... | collective-permute-start | bytes 12296 | tf_op jit(solution)/shard_map/ppermute | solution.py:24
  162.2 8.0 %collective-permute-start.28 = (f32[32,32]{1,0:T(8,128)S(1)}, f32[32,32]{1,0:T(8,128)S(1)}, u32[]{:S(2)}, u32[]{:S(2)}) collective-permute-start(f32[32,32]{1,0:T(8,128)S(1)} %add_add_fusion.5), channel_id=1, source_target_pairs={{128,0},{132,4},{136,8},{140,12},{144,16},{148,20},{152,24},{156,2... | collective-permute-start | bytes 12296 | tf_op jit(solution)/shard_map/ppermute | solution.py:24
  166.3 4.8 %collective-permute-start.29 = (f32[32,32]{1,0:T(8,128)S(1)}, f32[32,32]{1,0:T(8,128)S(1)}, u32[]{:S(2)}, u32[]{:S(2)}) collective-permute-start(f32[32,32]{1,0:T(8,128)S(1)} %add_add_fusion.5), channel_id=1, source_target_pairs={{192,0},{196,4},{200,8},{204,12},{208,16},{212,20},{216,24},{220,2... | collective-permute-start | bytes 12296 | tf_op jit(solution)/shard_map/ppermute | solution.py:24
  166.3 10.5 %collective-permute-start.34 = (f32[4,32,512]{2,1,0:T(8,128)S(1)}, f32[4,32,512]{2,1,0:T(8,128)S(1)}, u32[]{:S(2)}, u32[]{:S(2)}) collective-permute-start(f32[4,32,512]{2,1,0:T(8,128)S(1)} %pad_maximum_fusion.1), channel_id=1, source_target_pairs={{8,0},{12,4},{16,8},{20,12},{24,16},{28,20},{32,24},{36,28},{40,32... | collective-permute-start | bytes 786440 | tf_op jit(solution)/shard_map/ppermute | solution.py:24
  167.8 11.4 %collective-permute-start.35 = (f32[4,32,512]{2,1,0:T(8,128)S(1)}, f32[4,32,512]{2,1,0:T(8,128)S(1)}, u32[]{:S(2)}, u32[]{:S(2)}) collective-permute-start(f32[4,32,512]{2,1,0:T(8,128)S(1)} %pad_maximum_fusion.1), channel_id=1, source_target_pairs={{12,0},{16,4},{20,8},{24,12},{28,16},{32,20},{36,24},{40,28},{44,3... | collective-permute-start | bytes 786440 | tf_op jit(solution)/shard_map/ppermute | solution.py:24
  170.3 8.9 %collective-permute-start.36 = (f32[4,32,512]{2,1,0:T(8,128)S(1)}, f32[4,32,512]{2,1,0:T(8,128)S(1)}, u32[]{:S(2)}, u32[]{:S(2)}) collective-permute-start(f32[4,32,512]{2,1,0:T(8,128)S(1)} %pad_maximum_fusion.1), channel_id=1, source_target_pairs={{252,0},{0,4},{4,8},{8,12},{12,16},{16,20},{20,24},{24,28},{28,32}... | collective-permute-start | bytes 786440 | tf_op jit(solution)/shard_map/ppermute | solution.py:24
  171.1 17.0 %collective-permute-start.37 = (f32[4,32,512]{2,1,0:T(8,128)S(1)}, f32[4,32,512]{2,1,0:T(8,128)S(1)}, u32[]{:S(2)}, u32[]{:S(2)}) collective-permute-start(f32[4,32,512]{2,1,0:T(8,128)S(1)} %pad_maximum_fusion.1), channel_id=1, source_target_pairs={{248,0},{252,4},{0,8},{4,12},{8,16},{12,20},{16,24},{20,28},{24,32... | collective-permute-start | bytes 786440 | tf_op jit(solution)/shard_map/ppermute | solution.py:24
  172.4 20.2 %collective-permute-start.38 = (f32[4,32,512]{2,1,0:T(8,128)S(1)}, f32[4,32,512]{2,1,0:T(8,128)S(1)}, u32[]{:S(2)}, u32[]{:S(2)}) collective-permute-start(f32[4,32,512]{2,1,0:T(8,128)S(1)} %pad_maximum_fusion.1), channel_id=1, source_target_pairs={{244,0},{248,4},{252,8},{0,12},{4,16},{8,20},{12,24},{16,28},{20,3... | collective-permute-start | bytes 786440 | tf_op jit(solution)/shard_map/ppermute | solution.py:24
  206.2 3.7 %collective-permute-start.39 = (f32[32,32]{1,0:T(8,128)}, f32[32,32]{1,0:T(8,128)S(1)}, u32[]{:S(2)}, u32[]{:S(2)}) collective-permute-start(f32[32,32]{1,0:T(8,128)} %get-tuple-element.29), channel_id=1, source_target_pairs={{1,0},{2,1},{3,2},{0,3},{5,4},{6,5},{7,6},{4,7},{9,8},{10,9},{11,1... | collective-permute-start | bytes 12296 | tf_op jit(solution)/shard_map/ppermute | solution.py:24
  208.8 4.3 %collective-permute-start.40 = (f32[32,32]{1,0:T(8,128)}, f32[32,32]{1,0:T(8,128)S(1)}, u32[]{:S(2)}, u32[]{:S(2)}) collective-permute-start(f32[32,32]{1,0:T(8,128)} %get-tuple-element.29), channel_id=1, source_target_pairs={{2,0},{3,1},{0,2},{1,3},{6,4},{7,5},{4,6},{5,7},{10,8},{11,9},{8,1... | collective-permute-start | bytes 12296 | tf_op jit(solution)/shard_map/ppermute | solution.py:24
  209.4 4.2 %collective-permute-start.41 = (f32[32,32]{1,0:T(8,128)}, f32[32,32]{1,0:T(8,128)S(1)}, u32[]{:S(2)}, u32[]{:S(2)}) collective-permute-start(f32[32,32]{1,0:T(8,128)} %get-tuple-element.29), channel_id=1, source_target_pairs={{3,0},{0,1},{1,2},{2,3},{7,4},{4,5},{5,6},{6,7},{11,8},{8,9},{9,10... | collective-permute-start | bytes 12296 | tf_op jit(solution)/shard_map/ppermute | solution.py:24
  214.3 5.3 %collective-permute-start.42 = (f32[32,32]{1,0:T(8,128)S(1)}, f32[32,32]{1,0:T(8,128)S(1)}, u32[]{:S(2)}, u32[]{:S(2)}) collective-permute-start(f32[32,32]{1,0:T(8,128)S(1)} %add_add_fusion.3), channel_id=1, source_target_pairs={{4,0},{8,4},{12,8},{16,12},{20,16},{24,20},{28,24},{32,28},{36,32}... | collective-permute-start | bytes 12296 | tf_op jit(solution)/shard_map/ppermute | solution.py:24
  214.3 5.3 %collective-permute-start.43 = (f32[32,32]{1,0:T(8,128)S(1)}, f32[32,32]{1,0:T(8,128)S(1)}, u32[]{:S(2)}, u32[]{:S(2)}) collective-permute-start(f32[32,32]{1,0:T(8,128)S(1)} %add_add_fusion.3), channel_id=1, source_target_pairs={{8,0},{12,4},{16,8},{20,12},{24,16},{28,20},{32,24},{36,28},{40,32... | collective-permute-start | bytes 12296 | tf_op jit(solution)/shard_map/ppermute | solution.py:24
  216.1 5.3 %collective-permute-start.44 = (f32[32,32]{1,0:T(8,128)S(1)}, f32[32,32]{1,0:T(8,128)S(1)}, u32[]{:S(2)}, u32[]{:S(2)}) collective-permute-start(f32[32,32]{1,0:T(8,128)S(1)} %add_add_fusion.3), channel_id=1, source_target_pairs={{12,0},{16,4},{20,8},{24,12},{28,16},{32,20},{36,24},{40,28},{44,3... | collective-permute-start | bytes 12296 | tf_op jit(solution)/shard_map/ppermute | solution.py:24
  221.3 5.8 %collective-permute-start.45 = (f32[32,32]{1,0:T(8,128)S(1)}, f32[32,32]{1,0:T(8,128)S(1)}, u32[]{:S(2)}, u32[]{:S(2)}) collective-permute-start(f32[32,32]{1,0:T(8,128)S(1)} %add_add_fusion.2), channel_id=1, source_target_pairs={{16,0},{20,4},{24,8},{28,12},{32,16},{36,20},{40,24},{44,28},{48,3... | collective-permute-start | bytes 12296 | tf_op jit(solution)/shard_map/ppermute | solution.py:24
  226.6 5.0 %collective-permute-start.47 = (f32[32,32]{1,0:T(8,128)S(1)}, f32[32,32]{1,0:T(8,128)S(1)}, u32[]{:S(2)}, u32[]{:S(2)}) collective-permute-start(f32[32,32]{1,0:T(8,128)S(1)} %add_add_fusion.2), channel_id=1, source_target_pairs={{48,0},{52,4},{56,8},{60,12},{64,16},{68,20},{72,24},{76,28},{80,3... | collective-permute-start | bytes 12296 | tf_op jit(solution)/shard_map/ppermute | solution.py:24
  231.6 6.6 %collective-permute-start.48 = (f32[32,32]{1,0:T(8,128)S(1)}, f32[32,32]{1,0:T(8,128)S(1)}, u32[]{:S(2)}, u32[]{:S(2)}) collective-permute-start(f32[32,32]{1,0:T(8,128)S(1)} %add_add_fusion.1), channel_id=1, source_target_pairs={{64,0},{68,4},{72,8},{76,12},{80,16},{84,20},{88,24},{92,28},{96,3... | collective-permute-start | bytes 12296 | tf_op jit(solution)/shard_map/ppermute | solution.py:24
  235.6 6.6 %collective-permute-start.49 = (f32[32,32]{1,0:T(8,128)S(1)}, f32[32,32]{1,0:T(8,128)S(1)}, u32[]{:S(2)}, u32[]{:S(2)}) collective-permute-start(f32[32,32]{1,0:T(8,128)S(1)} %add_add_fusion.1), channel_id=1, source_target_pairs={{128,0},{132,4},{136,8},{140,12},{144,16},{148,20},{152,24},{156,2... | collective-permute-start | bytes 12296 | tf_op jit(solution)/shard_map/ppermute | solution.py:24
  236.1 6.2 %collective-permute-start.50 = (f32[32,32]{1,0:T(8,128)S(1)}, f32[32,32]{1,0:T(8,128)S(1)}, u32[]{:S(2)}, u32[]{:S(2)}) collective-permute-start(f32[32,32]{1,0:T(8,128)S(1)} %add_add_fusion.1), channel_id=1, source_target_pairs={{192,0},{196,4},{200,8},{204,12},{208,16},{212,20},{216,24},{220,2... | collective-permute-start | bytes 12296 | tf_op jit(solution)/shard_map/ppermute | solution.py:24
  (8 other events, 101.2 us)
